TPU v7x, 32 devices: a whole 2x2x4 slice. The times are simulated.
32 devices in a mesh: ctx: 8 (over z, core), tp: 4 (over y, x).
Axes of the slice: x: 2, y: 2, z: 4, core: 2. Of those that a mesh axis runs over, the one named last changes fastest.
Arguments:
- query_latent: bfloat16 [4096, 64, 512], P('ctx', 'tp'), may hold values from -24 to 24
- query_rope: bfloat16 [4096, 4096], P('ctx', 'tp'), may hold values from -24 to 24
- key_latent: bfloat16 [4096, 512], P('ctx'), may hold values from -6 to 6
- key_rope: bfloat16 [2048, 128], P('ctx'), may hold values from -6 to 6
- block_ids: int32 [16], replicated, may hold values from 0 to 15, as said below
- value_up: bfloat16 [64, 512, 128], P('tp'), may hold values from -0.5 to 0.5
- out_weight: bfloat16 [8192, 7168], P('tp'), may hold values from -0.0625 to 0.0625
- residual: bfloat16 [4096, 7168], P(('ctx', 'tp')), may hold values from -18 to 18
- norm_gain: float32 [7168], replicated, may hold values from 0.1 to 1.9
- gate_weight: bfloat16 [7168, 2048], P('ctx', 'tp'), may hold values from -0.0625 to 0.0625
- up_weight: bfloat16 [7168, 2048], P('ctx', 'tp'), may hold values from -0.0625 to 0.0625
- down_weight: bfloat16 [7168, 2048], P('ctx', 'tp'), may hold values from -0.125 to 0.125
Outputs:
- layer_out: bfloat16 [4096, 7168], P(('ctx', 'tp'))
Inputs may be any that keep to these rules, and one draw needn't show every extreme that they name: `block_ids`: index c of ctx stores blocks 2c and 2c + 1; their two entries sum to 15, and every value appears once.
All inputs are finite; a program needn't handle non-finite values.
Results may differ from a plain program's by a relative error of at most 0.018.
Values may be sent and summed in bfloat16 or wider, within the bound.
A program may use at most 192 MiB of HBM per device.

v0:
```python
import jax
import jax.numpy as jnp
from jax import lax
from jax.sharding import PartitionSpec as P


def from_behind(x, axis, by):
    length = lax.axis_size(axis)
    return lax.ppermute(x, axis, [(i, (i + by) % length) for i in range(length)])


def rms_norm(activation, gain_vector):
    mean_square = jnp.mean(activation * activation, axis=-1, keepdims=True)
    return (activation * lax.rsqrt(mean_square + 1e-06) * gain_vector).astype(jnp.bfloat16)


def local(
    query_latent,
    query_rope,
    key_latent,
    key_rope,
    block_ids,
    value_up,
    out_weight,
    residual,
    norm_gain,
    gate_weight,
    up_weight,
    down_weight,
):
    seq_rows = key_latent.shape[0]
    half_len = seq_rows // 2
    head_count = query_latent.shape[1]
    rope_dim = key_rope.shape[1] // 2
    head_dim = value_up.shape[2]
    ctx_count = lax.axis_size("ctx")
    tp_count = lax.axis_size("tp")
    score_scale = (head_dim + rope_dim) ** (-0.5)
    recv_latent, recv_rope = from_behind((key_latent, key_rope), "ctx", 1)
    keys_lat = jnp.concatenate([key_latent, recv_latent], axis=0)
    keys_rot = jnp.concatenate(
        [key_rope.reshape(seq_rows, rope_dim), recv_rope.reshape(seq_rows, rope_dim)], axis=0
    )
    current = lax.axis_index("ctx")
    previous = (current + ctx_count - 1) % ctx_count
    own_ids = lax.dynamic_slice_in_dim(block_ids, current * 2, 2, 0)
    prev_ids = lax.dynamic_slice_in_dim(block_ids, previous * 2, 2, 0)
    row_index = jnp.arange(seq_rows, dtype=jnp.int32)
    first_half = row_index < half_len
    offset = row_index % half_len
    query_pos = jnp.where(first_half, own_ids[0], own_ids[1]) * half_len + offset
    key_pos = jnp.concatenate(
        [query_pos, jnp.where(first_half, prev_ids[0], prev_ids[1]) * half_len + offset], axis=0
    )
    rope_queries = query_rope.reshape(seq_rows, head_count, rope_dim)
    block_rows = min(seq_rows, 512)

    def attend(block_index):
        scores = jnp.einsum(
            "shl,kl->hsk", query_latent, keys_lat, preferred_element_type=jnp.float32
        )
        scores = scores + jnp.einsum(
            "shr,kr->hsk", rope_queries, keys_rot, preferred_element_type=jnp.float32
        )
        scores = scores * score_scale
        visible = key_pos[None, :] <= query_pos[:, None]
        scores = jnp.where(visible[None], scores, -jnp.inf)
        highest = jnp.max(scores, axis=-1, keepdims=True)
        exponent = jnp.exp(scores - highest)
        weights = (exponent / jnp.sum(exponent, axis=-1, keepdims=True)).astype(jnp.bfloat16)
        blended = jnp.einsum(
            "hsk,kl->shl", weights, keys_lat, preferred_element_type=jnp.float32
        ).astype(jnp.bfloat16)
        values = jnp.einsum(
            "shl,hlv->shv", blended, value_up, preferred_element_type=jnp.float32
        ).astype(jnp.bfloat16)
        return values.reshape(block_rows, head_count * head_dim)

    head_out = lax.map(attend, jnp.arange(seq_rows // block_rows, dtype=jnp.int32)).reshape(
        seq_rows, head_count * head_dim
    )
    share_rows = seq_rows // tp_count
    tp_index = lax.axis_index("tp")
    partial_attn = jnp.dot(head_out, out_weight, preferred_element_type=jnp.float32)
    attn_total = lax.psum(partial_attn.astype(jnp.bfloat16), "tp").astype(jnp.float32)
    all_residual = lax.all_gather(residual, "tp", axis=0, tiled=True)
    hidden_state = all_residual.astype(jnp.float32) + attn_total
    normed_all = rms_norm(hidden_state, norm_gain)
    own_state = lax.dynamic_slice_in_dim(hidden_state, tp_index * share_rows, share_rows, 0)
    gate_full, up_full, down_full = (
        lax.all_gather(gate_weight, "ctx", axis=0, tiled=True),
        lax.all_gather(up_weight, "ctx", axis=0, tiled=True),
        lax.all_gather(down_weight, "ctx", axis=0, tiled=True),
    )
    gate_proj = jnp.dot(normed_all, gate_full, preferred_element_type=jnp.float32)
    up_proj = jnp.dot(normed_all, up_full, preferred_element_type=jnp.float32)
    hidden_units = (jax.nn.silu(gate_proj) * up_proj).astype(jnp.bfloat16)
    shared_part = lax.psum_scatter(
        lax.dot_general(
            hidden_units, down_full, (((1,), (1,)), ((), ())), preferred_element_type=jnp.float32
        ).astype(jnp.bfloat16),
        "tp",
        scatter_dimension=0,
        tiled=True,
    ).astype(jnp.float32)
    return (own_state + shared_part).astype(jnp.bfloat16)


def solution(mesh):
    placed = (
        P("ctx", "tp", None),
        P("ctx", "tp"),
        P("ctx", None),
        P("ctx", None),
        P(),
        P("tp", None, None),
        P("tp", None),
        P(("ctx", "tp"), None),
        P(),
        P("ctx", "tp"),
        P("ctx", "tp"),
        P("ctx", "tp"),
    )
    return jax.shard_map(
        local, mesh=mesh, in_specs=placed, out_specs=P(("ctx", "tp"), None), check_vma=False
    )
```

profile of v0, /device:TPU:0, one launch (start us, length us, event | category | flops | bytes accessed | tf_op | source)
XLA Modules:
  0.0 672.1 jit_solution(7638917272089841626)
XLA Ops:
  6.5 0.5 collective-permute-start
  7.0 2.7 collective-permute-start.1
  9.7 0.8 fusion.35
  10.5 0.6 fusion.34
  11.1 1.2 fusion.22
  12.3 1.3 multiply_add_fusion
  13.6 1.2 broadcast_compare_fusion
  14.8 0.9 reshape.69
  15.7 1.5 copy.19
  17.2 0.1 copy.17
  17.3 1.5 collective-permute-done.1
  18.8 0.1 reshape.70
  18.9 0.1 copy.18
  19.0 18.1 %fusion.3 = f32[1024,512,16]{1,0,2:T(8,128)} fusion(bf16[512,16,512]{2,1,0:T(8,128)(2,1)} %param.12, bf16[512,512]{1,0:T(8,128)(2,1)} %collective-permute-done, bf16[512,512]{1,0:T(8,128)(2,1)} %param.14), kind=kOutput, calls=%fused_computation.11 | convolution fusion | flops 8592031744 | bytes 42991616 | tf_op jit(solution)/shard_map/while/body/eval_jaxpr/shl,kl->hsk/dot_general | solution.py:59
  37.1 24.3 %fusion.37 = (f32[16,512]{1,0:T(8,128)S(1)}, f32[16,512,1024]{1,2,0:T(8,128)}) fusion(f32[1024,512,16]{1,0,2:T(8,128)} %fusion.3, pred[512,1024]{0,1:T(8,128)(4,1)} %broadcast_compare_fusion, bf16[512,16,64]{0,2,1:T(8,128)(2,1)S(1)} %bitcast.36, bf16[512,64]{0,1:T(8,128)(2,1)S(1)} %copy.18, bf16[512,64]{0,1:T(8,128)(2,1)S(1)} %copy.17), kind=kOutput, calls=%fused_computation.51 | convolution fusion | flops 1115948032 | bytes 68845568 | tf_op jit(solution)/shard_map/while/body/eval_jaxpr/sub | solution.py:69
  61.3 17.5 %fusion.9 = bf16[16,512,128]{1,2,0:T(8,128)(2,1)} fusion(bf16[16,512,128]{2,1,0:T(8,128)(2,1)S(1)} %copy-done, f32[16,512,1024]{1,2,0:T(8,128)} %get-tuple-element.41, f32[16,512]{1,0:T(8,128)S(1)} %get-tuple-element.40, bf16[512,512]{1,0:T(8,128)(2,1)} %collective-permute-done, bf16[512,512]{1,0:T(8,128)(2,1)} %param.14), kind=kOutput, calls=%fused_computation.17 | convolution fusion | flops 9687793664 | bytes 38830080 | tf_op jit(solution)/shard_map/while/body/eval_jaxpr/shl,hlv->shv/dot_general | solution.py:74
  78.9 23.3 %convolution_convert_fusion.1 = bf16[512,7168]{1,0:T(8,128)(2,1)} fusion(bf16[512,2048]{0,1:T(8,128)(2,1)} %bitcast.37, bf16[2048,7168]{1,0:T(8,128)(2,1)} %param.18), kind=kOutput, calls=%fused_computation.10 | convolution fusion | flops 15036055552 | bytes 38797312 | tf_op jit(solution)/shard_map/dot_general | solution.py:84
  102.2 0.0 all-gather.5.cloned.1.call-start
  102.3 0.7 all-gather.5.cloned.1.call-update
  103.0 0.7 all-gather.7.cloned.1.call-update
  103.7 0.5 all-gather.11.cloned.1.call-update
  104.3 0.5 all-gather.9.cloned.1.call-update
  104.9 153.2 %all-reduce.2.cloned.1.call-done = bf16[512,7168]{1,0:T(8,128)(2,1)} async-done(((bf16[512,7168]{1,0:T(8,128)(2,1)}), bf16[512,7168]{1,0:T(8,128)(2,1)}) %all-reduce.2.cloned.1.call-update) | async-done | bytes 7340048 | tf_op jit(solution)/shard_map/psum | solution.py:85
  258.1 80.8 %all-gather.5.cloned.1.call-done = bf16[512,7168]{1,0:T(8,128)(2,1)} async-done(((bf16[128,7168]{1,0:T(8,128)(2,1)}), bf16[512,7168]{1,0:T(8,128)(2,1)}) %all-gather.5.cloned.1.call-update) | async-done | bytes 7340048 | tf_op jit(solution)/shard_map/all_gather | solution.py:86
  338.9 13.5 %convert_add_fusion = (f32[512,7168]{1,0:T(8,128)}, f32[512]{0:T(512)S(1)}) fusion(bf16[512,7168]{1,0:T(8,128)(2,1)} %all-reduce.2.cloned.1.call-done, bf16[512,7168]{1,0:T(8,128)(2,1)} %all-gather.5.cloned.1.call-done), kind=kLoop, calls=%fused_computation.7 | loop fusion | flops 18349568 | bytes 29362176 | tf_op jit(solution)/shard_map/add | solution.py:87
  352.4 61.6 %all-gather.7.cloned.1.call-done = bf16[7168,512]{1,0:T(8,128)(2,1)} async-done(((bf16[896,512]{1,0:T(8,128)(2,1)}), bf16[7168,512]{1,0:T(8,128)(2,1)}) %all-gather.7.cloned.1.call-update) | async-done | bytes 7340048 | tf_op jit(solution)/shard_map/all_gather | solution.py:91
  413.9 9.7 %fusion.33 = f32[512,512]{1,0:T(8,128)S(1)} fusion(bf16[7168,512]{1,0:T(8,128)(2,1)} %all-gather.7.cloned.1.call-done, f32[7168]{0:T(1024)S(1)} %copy-done.2, f32[512]{0:T(512)S(1)} %add_rsqrt_fusion, bf16[512,7168]{1,0:T(8,128)(2,1)} %all-reduce.2.cloned.1.call-done, bf16[512,7168]{1,0:T(8,128)(2,1)} %all-gather.5.cloned.1.call-done), kind=kOutput, calls=%fused_computation.47 | convolution fusion | flops 3780116480 | bytes 23099392 | tf_op jit(solution)/shard_map/dot_general | solution.py:95
  423.7 63.8 %all-gather.11.cloned.1.call-done = bf16[7168,512]{1,0:T(8,128)(2,1)} async-done(((bf16[896,512]{1,0:T(8,128)(2,1)}), bf16[7168,512]{1,0:T(8,128)(2,1)}) %all-gather.11.cloned.1.call-update) | async-done | bytes 7340048 | tf_op jit(solution)/shard_map/all_gather | solution.py:93
  487.5 73.5 %all-gather.9.cloned.1.call-done = bf16[7168,512]{1,0:T(8,128)(2,1)} async-done(((bf16[896,512]{1,0:T(8,128)(2,1)}), bf16[7168,512]{1,0:T(8,128)(2,1)}) %all-gather.9.cloned.1.call-update) | async-done | bytes 7340048 | tf_op jit(solution)/shard_map/all_gather | solution.py:92
  561.0 22.3 %convolution_convert_fusion = bf16[512,7168]{1,0:T(8,128)(2,1)} fusion(bf16[7168,512]{1,0:T(8,128)(2,1)} %all-gather.11.cloned.1.call-done, bf16[7168,512]{1,0:T(8,128)(2,1)} %all-gather.9.cloned.1.call-done, f32[512,512]{1,0:T(8,128)S(1)} %fusion.33, f32[7168]{0:T(1024)S(1)} %copy-done.2, f32[512]{0:T(512)S(1)} %add_rsqrt_fusion, ...), kind=kOutput, calls=%fused_computation.9 | convolution fusion | flops 7543455744 | bytes 37779456 | tf_op jit(solution)/shard_map/dot_general | solution.py:99
  583.3 77.7 %reduce-scatter.2.cloned.1.call-done = bf16[128,7168]{1,0:T(8,128)(2,1)} async-done(((bf16[512,7168]{1,0:T(8,128)(2,1)}), bf16[128,7168]{1,0:T(8,128)(2,1)}) %reduce-scatter.2.cloned.1.call-update) | async-done | bytes 1835024 | tf_op jit(solution)/shard_map/reduce_scatter | solution.py:98
  661.1 4.2 add_convert_fusion
  (16 shorter events, 0.2 us)
Async XLA Ops:
  6.5 54.8 %copy-start = (bf16[16,512,128]{2,1,0:T(8,128)(2,1)S(1)}, bf16[16,512,128]{2,1,0:T(8,128)(2,1)}, u32[]{:S(2)}) copy-start(bf16[16,512,128]{2,1,0:T(8,128)(2,1)} %param.17) | copy-start | bytes 6291460
  6.5 251.6 %all-reduce.2.cloned.1.call-start = ((), (), s32[]{:S(2)}) async-start(), calls=%async_computation.2 | async-start | bytes 14680064 | tf_op jit(solution)/shard_map/psum | solution.py:85
  6.5 12.5 %collective-permute-start = (bf16[512,512]{1,0:T(8,128)(2,1)}, bf16[512,512]{1,0:T(8,128)(2,1)}, u32[]{:S(2)}, u32[]{:S(2)}) collective-permute-start(bf16[512,512]{1,0:T(8,128)(2,1)} %param.14), channel_id=1, source_target_pairs={{0,4},{4,8},{8,12},{12,16},{16,20},{20,24},{24,28},{28,0},{1,5},{5... | collective-permute-start | bytes 1572872 | tf_op jit(solution)/shard_map/ppermute | solution.py:9
  7.0 11.8 %collective-permute-start.1 = (bf16[256,128]{1,0:T(8,128)(2,1)}, bf16[256,128]{1,0:T(8,128)(2,1)S(1)}, u32[]{:S(2)}, u32[]{:S(2)}) collective-permute-start(bf16[256,128]{1,0:T(8,128)(2,1)} %param.15), channel_id=1, source_target_pairs={{0,4},{4,8},{8,12},{12,16},{16,20},{20,24},{24,28},{28,0},{1,5},{5... | collective-permute-start | bytes 196616 | tf_op jit(solution)/shard_map/ppermute | solution.py:9
  102.2 236.6 %all-gather.5.cloned.1.call-start = ((), (), s32[]{:S(2)}) async-start(), calls=%async_computation.1 | async-start | bytes 9175040 | tf_op jit(solution)/shard_map/all_gather | solution.py:86
  103.0 311.0 %all-gather.7.cloned.1.call-start = ((), (), s32[]{:S(2)}) async-start(), calls=%async_computation.3 | async-start | bytes 8257536 | tf_op jit(solution)/shard_map/all_gather | solution.py:91
  103.7 383.8 %all-gather.11.cloned.1.call-start = ((), (), s32[]{:S(2)}) async-start(), calls=%async_computation.5 | async-start | bytes 8257536 | tf_op jit(solution)/shard_map/all_gather | solution.py:93
  104.3 456.7 %all-gather.9.cloned.1.call-start = ((), (), s32[]{:S(2)}) async-start(), calls=%async_computation.4 | async-start | bytes 8257536 | tf_op jit(solution)/shard_map/all_gather | solution.py:92
  104.9 309.1 %copy-start.2 = (f32[7168]{0:T(1024)S(1)}, f32[7168]{0:T(1024)}, u32[]{:S(2)}) copy-start(f32[7168]{0:T(1024)} %param.20) | copy-start | bytes 86020
  104.9 556.2 %reduce-scatter.2.cloned.1.call-start = ((), (), s32[]{:S(2)}) async-start(), calls=%async_computation.6 | async-start | bytes 9175040 | tf_op jit(solution)/shard_map/reduce_scatter | solution.py:98
  583.3 81.9 %copy-start.1 = (bf16[16,512,128]{2,1,0:T(8,128)(2,1)S(1)}, bf16[16,512,128]{2,1,0:T(8,128)(2,1)}, u32[]{:S(2)}) copy-start(bf16[16,512,128]{2,1,0:T(8,128)(2,1)} %param.17) | copy-start | bytes 6291460
Sparse Core Ops, SparseCore 0:
  102.3 155.7 all-reduce.1
  259.9 78.8 all-gather.4
  340.5 73.3 all-gather.6
  415.4 71.9 all-gather.10
  489.0 71.9 all-gather.8
  583.5 77.5 reduce-scatter.1
where the time goes:
time: 672 us
  waiting for transfers between devices  515 us (77%)
  matrix products  115 us (17%)
  other arithmetic  21.3 us (3%)
  between operations  13.6 us (2%)
    psum x1, waiting for transfers between devices, local(): lax.psum(partial_attn.astype(jnp.bfloat16), 'tp').astype(jnp.float32)  153 us
    all_gather x1, waiting for transfers between devices, local(): all_residual = lax.all_gather(residual, 'tp', axis=0, tiled=True)  80.8 us
    reduce_scatter x1, waiting for transfers between devices, local(): lax.psum_scatter(lax.dot_general(hidden_units, down_full, (((1,), (1,)),...  77.7 us
    all_gather x1, waiting for transfers between devices, local(): lax.all_gather(up_weight, 'ctx', axis=0, tiled=True)  73.5 us
    all_gather x1, waiting for transfers between devices, local(): lax.all_gather(down_weight, 'ctx', axis=0, tiled=True)  63.8 us
    all_gather x1, waiting for transfers between devices, local(): lax.all_gather(gate_weight, 'ctx', axis=0, tiled=True)  61.6 us
    sub x1, matrix products, attend(): exponent = jnp.exp(scores - highest)  24.3 us
    dot_general x1, matrix products, local(): jnp.dot(head_out, out_weight, preferred_element_type=jnp.float32)  23.3 us
  transfers between devices with their start and end apart: 8, of which 7 were waited for; matrix products, arithmetic and copies ran while one was open for 5% of the time, Pallas kernels for 0%

commit v1 on v0

--- a/solution.py
+++ b/solution.py
@@ -2,6 +2,27 @@
 import jax.numpy as jnp
 from jax import lax
 from jax.sharding import PartitionSpec as P
+
+
+def ring_gather(x, axis, dim):
+    size, place, rows = (lax.axis_size(axis), lax.axis_index(axis), x.shape[dim])
+    upward = [(i, (i + 1) % size) for i in range(size)]
+    left = [(i, (i - 1) % size) for i in range(size)]
+    out = jnp.zeros((*x.shape[:dim], size * rows, *x.shape[dim + 1 :]), x.dtype)
+    out = lax.dynamic_update_slice_in_dim(out, x, place * rows, axis=dim)
+    from_left = from_right = x
+    halfway = size // 2
+    for step in range(1, halfway + 1):
+        from_left = lax.ppermute(from_left, axis, upward)
+        out = lax.dynamic_update_slice_in_dim(
+            out, from_left, (place - step) % size * rows, axis=dim
+        )
+        if step < size - halfway:
+            from_right = lax.ppermute(from_right, axis, left)
+            out = lax.dynamic_update_slice_in_dim(
+                out, from_right, (place + step) % size * rows, axis=dim
+            )
+    return out
 
 
 def from_behind(x, axis, by):
@@ -88,7 +109,7 @@
     normed_all = rms_norm(hidden_state, norm_gain)
     own_state = lax.dynamic_slice_in_dim(hidden_state, tp_index * share_rows, share_rows, 0)
     gate_full, up_full, down_full = (
-        lax.all_gather(gate_weight, "ctx", axis=0, tiled=True),
+        ring_gather(gate_weight, "ctx", 0),
         lax.all_gather(up_weight, "ctx", axis=0, tiled=True),
         lax.all_gather(down_weight, "ctx", axis=0, tiled=True),
     )

time: 672 us -> 599 us (0.89)
  waiting for transfers between devices: 515 us -> 414 us
  local copies, waits for them, and re-layouts: 4.16 us -> 20.7 us
  starting transfers between devices: 3.33 us -> 14 us
    psum x1, waiting for transfers between devices: 153 us -> 66.8 us  [local(): lax.psum(partial_attn.astype(jnp.bfloat16), 'tp').astype(jnp.float32)]
    all_gather x1 -> x0, waiting for transfers between devices: 61.6 us -> none  [local(): lax.all_gather(gate_weight, 'ctx', axis=0, tiled=True)]
    ppermute x0 -> x7, waiting for transfers between devices: none -> 59.7 us  [the longest x4 59.7 us: ring_gather(): from_left = lax.ppermute(from_left, axis, upward)]
    dynamic_update_slice x0 -> x8, local copies, waits for them, and re-layouts: none -> 13 us  [the longest x4 6.5 us: ring_gather(): lax.dynamic_update_slice_in_dim(out, from_left, (place - step) % size * r...]
    all_gather x1, waiting for transfers between devices: 73.5 us -> 61.6 us  [local(): lax.all_gather(up_weight, 'ctx', axis=0, tiled=True)]
    ppermute x0 -> x7, starting transfers between devices: none -> 10.7 us  [the longest x3 10.6 us: ring_gather(): from_right = lax.ppermute(from_right, axis, left)]
  transfers between devices with their start and end apart: 8 -> 14, of which waited for: 7 -> 9; matrix products, arithmetic and copies ran while one was open for 5% -> 8% of each run, Pallas kernels for 0% -> 0%
where the time goes in v1:
time: 599 us; the launch traced here: 598 us
  waiting for transfers between devices  414 us (69%)
  matrix products  115 us (19%)
  other arithmetic  21.4 us (4%)
  local copies, waits for them, and re-layouts  20.7 us (3%)
  starting transfers between devices  14 us (2%)
  between operations  13.3 us (2%)
    all_gather x1, waiting for transfers between devices, local(): all_residual = lax.all_gather(residual, 'tp', axis=0, tiled=True)  80.8 us
    reduce_scatter x1, waiting for transfers between devices, local(): lax.psum_scatter(lax.dot_general(hidden_units, down_full, (((1,), (1,)),...  77.7 us
    psum x1, waiting for transfers between devices, local(): lax.psum(partial_attn.astype(jnp.bfloat16), 'tp').astype(jnp.float32)  66.8 us
    all_gather x1, waiting for transfers between devices, local(): lax.all_gather(down_weight, 'ctx', axis=0, tiled=True)  63.8 us
    all_gather x1, waiting for transfers between devices, local(): lax.all_gather(up_weight, 'ctx', axis=0, tiled=True)  61.6 us
    ppermute x4, waiting for transfers between devices, ring_gather(): from_left = lax.ppermute(from_left, axis, upward)  59.7 us
    sub x1, matrix products, attend(): exponent = jnp.exp(scores - highest)  24.3 us
    dot_general x1, matrix products, local(): jnp.dot(head_out, out_weight, preferred_element_type=jnp.float32)  23.3 us
  transfers between devices with their start and end apart: 14, of which 9 were waited for; matrix products, arithmetic and copies ran while one was open for 8% of the time, Pallas kernels for 0%

profile of v1, /device:TPU:0, one launch (start us, length us, event | category | flops | bytes accessed | tf_op | source)
XLA Modules:
  0.0 598.3 jit_solution(13329576980836910883)
XLA Ops:
  7.0 2.7 collective-permute-start.1
  11.2 1.4 fusion.16
  12.5 1.2 multiply_add_fusion
  13.8 1.2 broadcast_compare_fusion
  15.9 1.5 copy.19
  17.5 1.3 collective-permute-done.1
  19.0 18.0 %fusion.3 = f32[1024,512,16]{1,0,2:T(8,128)} fusion(bf16[512,16,512]{2,1,0:T(8,128)(2,1)} %param.12, bf16[512,512]{1,0:T(8,128)(2,1)} %collective-permute-done, bf16[512,512]{1,0:T(8,128)(2,1)} %param.14), kind=kOutput, calls=%fused_computation.11 | convolution fusion | flops 8592031744 | bytes 42991616 | tf_op jit(solution)/shard_map/while/body/eval_jaxpr/shl,kl->hsk/dot_general | solution.py:80
  37.1 24.3 %fusion.32 = (f32[16,512]{1,0:T(8,128)S(1)}, f32[16,512,1024]{1,2,0:T(8,128)}) fusion(f32[1024,512,16]{1,0,2:T(8,128)} %fusion.3, pred[512,1024]{0,1:T(8,128)(4,1)} %broadcast_compare_fusion, bf16[512,16,64]{0,2,1:T(8,128)(2,1)S(1)} %bitcast.36, bf16[512,64]{0,1:T(8,128)(2,1)S(1)} %copy.18, bf16[512,64]{0,1:T(8,128)(2,1)S(1)} %copy.17), kind=kOutput, calls=%fused_computation.54 | convolution fusion | flops 1115948032 | bytes 68845568 | tf_op jit(solution)/shard_map/while/body/eval_jaxpr/sub | solution.py:90
  61.3 17.5 %fusion.9 = bf16[16,512,128]{1,2,0:T(8,128)(2,1)} fusion(bf16[16,512,128]{2,1,0:T(8,128)(2,1)S(1)} %copy-done, f32[16,512,1024]{1,2,0:T(8,128)} %get-tuple-element.41, f32[16,512]{1,0:T(8,128)S(1)} %get-tuple-element.40, bf16[512,512]{1,0:T(8,128)(2,1)} %collective-permute-done, bf16[512,512]{1,0:T(8,128)(2,1)} %param.14), kind=kOutput, calls=%fused_computation.17 | convolution fusion | flops 9687793664 | bytes 38830080 | tf_op jit(solution)/shard_map/while/body/eval_jaxpr/shl,hlv->shv/dot_general | solution.py:95
  78.9 23.3 %convolution_convert_fusion.1 = bf16[512,7168]{1,0:T(8,128)(2,1)} fusion(bf16[512,2048]{0,1:T(8,128)(2,1)} %bitcast.37, bf16[2048,7168]{1,0:T(8,128)(2,1)} %param.18), kind=kOutput, calls=%fused_computation.10 | convolution fusion | flops 15036055552 | bytes 38797312 | tf_op jit(solution)/shard_map/dot_general | solution.py:105
  104.4 3.5 collective-permute-start.3
  107.9 20.1 %collective-permute-done.2 = bf16[896,512]{1,0:T(8,128)(2,1)S(1)} collective-permute-done((bf16[896,512]{1,0:T(8,128)(2,1)S(1)}, bf16[896,512]{1,0:T(8,128)(2,1)S(1)}, u32[]{:S(2)}, u32[]{:S(2)}) %collective-permute-start.2) | collective-permute-done | bytes 917536 | tf_op jit(solution)/shard_map/ppermute | solution.py:16
  128.0 3.5 collective-permute-start.5
  131.5 20.4 %collective-permute-done.4 = bf16[896,512]{1,0:T(8,128)(2,1)} collective-permute-done((bf16[896,512]{1,0:T(8,128)(2,1)S(1)}, bf16[896,512]{1,0:T(8,128)(2,1)}, u32[]{:S(2)}, u32[]{:S(2)}) %collective-permute-start.4) | collective-permute-done | bytes 917536 | tf_op jit(solution)/shard_map/ppermute | solution.py:16
  152.0 3.5 collective-permute-start.7
  155.5 19.2 %collective-permute-done.6 = bf16[896,512]{1,0:T(8,128)(2,1)} collective-permute-done((bf16[896,512]{1,0:T(8,128)(2,1)}, bf16[896,512]{1,0:T(8,128)(2,1)}, u32[]{:S(2)}, u32[]{:S(2)}) %collective-permute-start.6) | collective-permute-done | bytes 917536 | tf_op jit(solution)/shard_map/ppermute | solution.py:16
  174.7 3.5 broadcast_in_dim.55
  179.2 1.0 constant_dynamic-update-slice_fusion.6
  181.1 2.2 constant_dynamic-update-slice_fusion.4
  183.3 2.2 constant_dynamic-update-slice_fusion.3
  185.5 2.3 constant_dynamic-update-slice_fusion.2
  187.8 2.4 constant_dynamic-update-slice_fusion.1
  190.2 1.0 constant_dynamic-update-slice_fusion
  191.2 66.8 %all-reduce.2.cloned.1.call-done = bf16[512,7168]{1,0:T(8,128)(2,1)} async-done(((bf16[512,7168]{1,0:T(8,128)(2,1)}), bf16[512,7168]{1,0:T(8,128)(2,1)}) %all-reduce.2.cloned.1.call-update) | async-done | bytes 7340048 | tf_op jit(solution)/shard_map/psum | solution.py:106
  258.1 80.8 %all-gather.4.cloned.1.call-done = bf16[512,7168]{1,0:T(8,128)(2,1)} async-done(((bf16[128,7168]{1,0:T(8,128)(2,1)}), bf16[512,7168]{1,0:T(8,128)(2,1)}) %all-gather.4.cloned.1.call-update) | async-done | bytes 7340048 | tf_op jit(solution)/shard_map/all_gather | solution.py:107
  338.8 13.5 %convert_add_fusion = (f32[512,7168]{1,0:T(8,128)}, f32[512]{0:T(512)S(1)}) fusion(bf16[512,7168]{1,0:T(8,128)(2,1)} %all-reduce.2.cloned.1.call-done, bf16[512,7168]{1,0:T(8,128)(2,1)} %all-gather.4.cloned.1.call-done), kind=kLoop, calls=%fused_computation.7 | loop fusion | flops 18349568 | bytes 29362176 | tf_op jit(solution)/shard_map/add | solution.py:108
  352.3 61.6 %all-gather.6.cloned.1.call-done = bf16[7168,512]{1,0:T(8,128)(2,1)} async-done(((bf16[896,512]{1,0:T(8,128)(2,1)}), bf16[7168,512]{1,0:T(8,128)(2,1)}) %all-gather.6.cloned.1.call-update) | async-done | bytes 7340048 | tf_op jit(solution)/shard_map/all_gather | solution.py:113
  413.9 9.7 %fusion.27 = f32[512,512]{1,0:T(8,128)S(1)} fusion(bf16[7168,512]{1,0:T(8,128)(2,1)} %all-gather.6.cloned.1.call-done, f32[7168]{0:T(1024)S(1)} %copy-done.3, f32[512]{0:T(512)S(1)} %add_rsqrt_fusion, bf16[512,7168]{1,0:T(8,128)(2,1)} %all-reduce.2.cloned.1.call-done, bf16[512,7168]{1,0:T(8,128)(2,1)} %all-gather.4.cloned.1.call-done), kind=kOutput, calls=%fused_computation.49 | convolution fusion | flops 3780116480 | bytes 23099392 | tf_op jit(solution)/shard_map/dot_general | solution.py:117
  423.6 63.8 %all-gather.8.cloned.1.call-done = bf16[7168,512]{1,0:T(8,128)(2,1)} async-done(((bf16[896,512]{1,0:T(8,128)(2,1)}), bf16[7168,512]{1,0:T(8,128)(2,1)}) %all-gather.8.cloned.1.call-update) | async-done | bytes 7340048 | tf_op jit(solution)/shard_map/all_gather | solution.py:114
  487.4 22.4 %convolution_convert_fusion = bf16[512,7168]{1,0:T(8,128)(2,1)} fusion(bf16[7168,512]{1,0:T(8,128)(2,1)} %all-gather.8.cloned.1.call-done, f32[512,512]{1,0:T(8,128)S(1)} %fusion.27, bf16[7168,512]{1,0:T(8,128)(2,1)} %constant_dynamic-update-slice_fusion, f32[7168]{0:T(1024)S(1)} %copy-done.3, f32[512]{0:T(512)S(1)} %add_rsqrt_fusion, ...), kind=kOutput, calls=%fused_computation.9 | convolution fusion | flops 7543455744 | bytes 37779456 | tf_op jit(solution)/shard_map/dot_general | solution.py:120
  509.9 77.7 %reduce-scatter.2.cloned.1.call-done = bf16[128,7168]{1,0:T(8,128)(2,1)} async-done(((bf16[512,7168]{1,0:T(8,128)(2,1)}), bf16[128,7168]{1,0:T(8,128)(2,1)}) %reduce-scatter.2.cloned.1.call-update) | async-done | bytes 1835024 | tf_op jit(solution)/shard_map/reduce_scatter | solution.py:119
  587.6 4.2 add_convert_fusion
  (38 shorter events, 7.3 us)
Async XLA Ops:
  6.5 54.8 %copy-start = (bf16[16,512,128]{2,1,0:T(8,128)(2,1)S(1)}, bf16[16,512,128]{2,1,0:T(8,128)(2,1)}, u32[]{:S(2)}) copy-start(bf16[16,512,128]{2,1,0:T(8,128)(2,1)} %param.17) | copy-start | bytes 6291460
  6.5 251.5 %all-reduce.2.cloned.1.call-start = ((), (), s32[]{:S(2)}) async-start(), calls=%async_computation.2 | async-start | bytes 14680064 | tf_op jit(solution)/shard_map/psum | solution.py:106
  6.5 12.5 %collective-permute-start = (bf16[512,512]{1,0:T(8,128)(2,1)}, bf16[512,512]{1,0:T(8,128)(2,1)}, u32[]{:S(2)}, u32[]{:S(2)}) collective-permute-start(bf16[512,512]{1,0:T(8,128)(2,1)} %param.14), channel_id=1, source_target_pairs={{0,4},{4,8},{8,12},{12,16},{16,20},{20,24},{24,28},{28,0},{1,5},{5... | collective-permute-start | bytes 1572872 | tf_op jit(solution)/shard_map/ppermute | solution.py:30
  7.0 11.8 %collective-permute-start.1 = (bf16[256,128]{1,0:T(8,128)(2,1)}, bf16[256,128]{1,0:T(8,128)(2,1)S(1)}, u32[]{:S(2)}, u32[]{:S(2)}) collective-permute-start(bf16[256,128]{1,0:T(8,128)(2,1)} %param.15), channel_id=1, source_target_pairs={{0,4},{4,8},{8,12},{12,16},{16,20},{20,24},{24,28},{28,0},{1,5},{5... | collective-permute-start | bytes 196616 | tf_op jit(solution)/shard_map/ppermute | solution.py:30
  102.2 2.1 copy-start.2
  102.2 236.6 %all-gather.4.cloned.1.call-start = ((), (), s32[]{:S(2)}) async-start(), calls=%async_computation.1 | async-start | bytes 9175040 | tf_op jit(solution)/shard_map/all_gather | solution.py:107
  102.9 311.0 %all-gather.6.cloned.1.call-start = ((), (), s32[]{:S(2)}) async-start(), calls=%async_computation.3 | async-start | bytes 8257536 | tf_op jit(solution)/shard_map/all_gather | solution.py:113
  103.7 383.8 %all-gather.8.cloned.1.call-start = ((), (), s32[]{:S(2)}) async-start(), calls=%async_computation.4 | async-start | bytes 8257536 | tf_op jit(solution)/shard_map/all_gather | solution.py:114
  104.2 483.4 %reduce-scatter.2.cloned.1.call-start = ((), (), s32[]{:S(2)}) async-start(), calls=%async_computation.5 | async-start | bytes 9175040 | tf_op jit(solution)/shard_map/reduce_scatter | solution.py:119
  104.3 23.7 %collective-permute-start.2 = (bf16[896,512]{1,0:T(8,128)(2,1)S(1)}, bf16[896,512]{1,0:T(8,128)(2,1)S(1)}, u32[]{:S(2)}, u32[]{:S(2)}) collective-permute-start(bf16[896,512]{1,0:T(8,128)(2,1)S(1)} %copy-done.2), channel_id=1, source_target_pairs={{0,4},{4,8},{8,12},{12,16},{16,20},{20,24},{24,28},{28,0},{1,5},{5... | collective-permute-start | bytes 2752520 | tf_op jit(solution)/shard_map/ppermute | solution.py:16
  104.4 23.6 %collective-permute-start.3 = (bf16[896,512]{1,0:T(8,128)(2,1)S(1)}, bf16[896,512]{1,0:T(8,128)(2,1)S(1)}, u32[]{:S(2)}, u32[]{:S(2)}) collective-permute-start(bf16[896,512]{1,0:T(8,128)(2,1)S(1)} %copy-done.2), channel_id=1, source_target_pairs={{0,28},{4,0},{8,4},{12,8},{16,12},{20,16},{24,20},{28,24},{1,29},{... | collective-permute-start | bytes 2752520 | tf_op jit(solution)/shard_map/ppermute | solution.py:21
  128.0 24.0 %collective-permute-start.4 = (bf16[896,512]{1,0:T(8,128)(2,1)S(1)}, bf16[896,512]{1,0:T(8,128)(2,1)}, u32[]{:S(2)}, u32[]{:S(2)}) collective-permute-start(bf16[896,512]{1,0:T(8,128)(2,1)S(1)} %collective-permute-done.2), channel_id=1, source_target_pairs={{0,4},{4,8},{8,12},{12,16},{16,20},{20,24},{24,28},{28,0},{1,5},{5... | collective-permute-start | bytes 2752520 | tf_op jit(solution)/shard_map/ppermute | solution.py:16
  128.0 24.0 %collective-permute-start.5 = (bf16[896,512]{1,0:T(8,128)(2,1)S(1)}, bf16[896,512]{1,0:T(8,128)(2,1)}, u32[]{:S(2)}, u32[]{:S(2)}) collective-permute-start(bf16[896,512]{1,0:T(8,128)(2,1)S(1)} %collective-permute-done.3), channel_id=1, source_target_pairs={{0,28},{4,0},{8,4},{12,8},{16,12},{20,16},{24,20},{28,24},{1,29},{... | collective-permute-start | bytes 2752520 | tf_op jit(solution)/shard_map/ppermute | solution.py:21
  152.0 22.7 %collective-permute-start.6 = (bf16[896,512]{1,0:T(8,128)(2,1)}, bf16[896,512]{1,0:T(8,128)(2,1)}, u32[]{:S(2)}, u32[]{:S(2)}) collective-permute-start(bf16[896,512]{1,0:T(8,128)(2,1)} %collective-permute-done.4), channel_id=1, source_target_pairs={{0,4},{4,8},{8,12},{12,16},{16,20},{20,24},{24,28},{28,0},{1,5},{5... | collective-permute-start | bytes 2752520 | tf_op jit(solution)/shard_map/ppermute | solution.py:16
  152.0 35.8 %collective-permute-start.7 = (bf16[896,512]{1,0:T(8,128)(2,1)}, bf16[896,512]{1,0:T(8,128)(2,1)}, u32[]{:S(2)}, u32[]{:S(2)}) collective-permute-start(bf16[896,512]{1,0:T(8,128)(2,1)} %collective-permute-done.5), channel_id=1, source_target_pairs={{0,28},{4,0},{8,4},{12,8},{16,12},{20,16},{24,20},{28,24},{1,29},{... | collective-permute-start | bytes 2752520 | tf_op jit(solution)/shard_map/ppermute | solution.py:21
  174.7 15.5 %collective-permute-start.8 = (bf16[896,512]{1,0:T(8,128)(2,1)}, bf16[896,512]{1,0:T(8,128)(2,1)S(1)}, u32[]{:S(2)}, u32[]{:S(2)}) collective-permute-start(bf16[896,512]{1,0:T(8,128)(2,1)} %collective-permute-done.6), channel_id=1, source_target_pairs={{0,4},{4,8},{8,12},{12,16},{16,20},{20,24},{24,28},{28,0},{1,5},{5... | collective-permute-start | bytes 2752520 | tf_op jit(solution)/shard_map/ppermute | solution.py:16
  191.2 222.7 %copy-start.3 = (f32[7168]{0:T(1024)S(1)}, f32[7168]{0:T(1024)}, u32[]{:S(2)}) copy-start(f32[7168]{0:T(1024)} %param.20) | copy-start | bytes 86020
  509.8 81.9 %copy-start.1 = (bf16[16,512,128]{2,1,0:T(8,128)(2,1)S(1)}, bf16[16,512,128]{2,1,0:T(8,128)(2,1)}, u32[]{:S(2)}) copy-start(bf16[16,512,128]{2,1,0:T(8,128)(2,1)} %param.17) | copy-start | bytes 6291460
Sparse Core Ops, SparseCore 0:
  102.3 155.7 all-reduce.1
  259.9 78.8 all-gather.3
  340.5 73.3 all-gather.5
  415.4 71.9 all-gather.7
  510.0 77.5 reduce-scatter.1
